TPU v7x, 256 devices: a whole 4x4x8 slice. The times are simulated.
256 devices in a mesh: section: 8 (over z), tile: 32 (over y, x, core).
Axes of the slice: x: 4, y: 4, z: 8, core: 2. Of those that a mesh axis runs over, the one named last changes fastest.
Arguments:
- frames_in: bfloat16 [16, 192, 96, 128], P(None, None, 'tile'), may hold values from -6 to 6
- norm_gain: float32 [8, 192], P('section'), may hold values from 0.1 to 1.9
- conv_weight: bfloat16 [8, 27, 192, 192], P('section'), may hold values from -0.078125 to 0.078125
- conv_bias: float32 [8, 192], P('section'), may hold values from -0.5 to 0.5
Outputs:
- decoded: bfloat16 [16, 192, 96, 128], P('section', None, 'tile')
All inputs are finite; a program needn't handle non-finite values.
Results may differ from a plain program's by a relative error of at most 0.017.
Values may be sent and summed in bfloat16 or wider, within the bound.
No kernel may reach another device: no remote copies, remote signals or barrier semaphores. Data moves between devices by JAX's collectives and lax.ppermute only.
A program may use at most 192 MiB of HBM per device.

v0:
```python
import jax
import jax.numpy as jnp
from jax import lax
from jax.sharding import PartitionSpec as P

GROUPS = 4
CF = 4


def padded_2(cells, sides, width):
    for axis, dim in sides:
        count = lax.axis_size(axis)
        ends = count - 1
        head = lax.slice_in_dim(cells, 0, width, axis=dim)
        tail = lax.slice_in_dim(cells, cells.shape[dim] - width, cells.shape[dim], axis=dim)
        cells = jnp.concatenate(
            [
                lax.ppermute(tail, axis, [(i, (i + 1) % count) for i in range(ends)]),
                cells,
                lax.ppermute(head, axis, [((i + 1) % count, i) for i in range(ends)]),
            ],
            axis=dim,
        )
    return cells


def shifted(value, axis, by):
    devices = lax.axis_size(axis)
    pairs = [(i, i + by) for i in range(devices) if 0 <= i + by < devices]
    return lax.ppermute(value, axis, pairs)


def broadcast(block, axis, source):
    block = jnp.where(lax.axis_index(axis) == source, block, jnp.zeros_like(block))
    return lax.psum(block, axis)


def normalize_act(current, gains):
    values = current.astype(jnp.float32)
    meansq = jnp.mean(values * values, axis=1, keepdims=True)
    normed = values * lax.rsqrt(meansq + 1e-06) * gains[None, :, None, None]
    return jax.nn.silu(normed).astype(jnp.bfloat16)


def apply_conv(stacked, weight_cat, frame_count, height, breadth):
    padded = jnp.pad(stacked, ((0, 0), (0, 0), (0, 0), (1, 1)))
    summed = jnp.zeros((frame_count, weight_cat.shape[1], height, breadth), jnp.float32)
    for time_off in range(3):
        pieces = [
            padded[
                time_off : time_off + frame_count,
                :,
                row_off : row_off + height,
                col_off : col_off + breadth,
            ]
            for row_off in range(3)
            for col_off in range(3)
        ]
        tap_stack = jnp.concatenate(pieces, axis=1)
        summed = summed + jnp.einsum(
            "ok,tkrw->torw", weight_cat[time_off], tap_stack, preferred_element_type=jnp.float32
        )
    return summed


def arrange_taps(taps, channels):
    return (
        taps.reshape(3, 9, channels, channels)
        .transpose(0, 2, 1, 3)
        .reshape(3, channels, 9 * channels)
    )


def on_device(frames_in, norm_gain, conv_weight, conv_bias):
    sections = lax.axis_size("section")
    my_section = lax.axis_index("section")
    channels = frames_in.shape[1]
    height = frames_in.shape[2]
    breadth = frames_in.shape[3]
    share = GROUPS * CF // sections
    group_input = frames_in.reshape(GROUPS, CF, channels, height, breadth)
    gains = norm_gain[0]
    biases = conv_bias[0]
    weight_cat = arrange_taps(conv_weight[0], channels)
    step_total = GROUPS + sections - 1
    group_shape = (CF, channels, height, breadth)
    cache_start = jnp.zeros((2, channels, height, breadth), jnp.bfloat16)
    arriving_start = jnp.zeros(group_shape, jnp.bfloat16)
    finished_start = jnp.zeros((GROUPS,) + group_shape, jnp.bfloat16)

    def advance(step, carry):
        arriving, cache, finished = carry
        position = step - my_section
        active = jnp.logical_and(position >= 0, position < GROUPS)
        safe_pos = jnp.clip(position, 0, GROUPS - 1)
        fresh = lax.dynamic_index_in_dim(group_input, safe_pos, 0, keepdims=False)
        current = jnp.where(my_section == 0, fresh, arriving)
        hidden = normalize_act(current, gains)
        stacked = padded_2(jnp.concatenate([cache, hidden], axis=0), (("tile", 2),), 1)
        renewed = hidden[CF - 2 :]
        update = lax.cond(
            active,
            lambda: apply_conv(stacked, weight_cat, CF, height, breadth),
            lambda: jnp.zeros(group_shape, jnp.float32),
        )
        result = (current.astype(jnp.float32) + update + biases[None, :, None, None]).astype(
            jnp.bfloat16
        )
        cache = jnp.where(active, renewed, cache)
        storing = jnp.logical_and(active, my_section == sections - 1)
        previous = lax.dynamic_index_in_dim(finished, safe_pos, 0, keepdims=False)
        finished = lax.dynamic_update_index_in_dim(
            finished, jnp.where(storing, result, previous), safe_pos, 0
        )
        arriving = shifted(result, "section", 1)
        return (arriving, cache, finished)

    arriving, cache, finished = lax.fori_loop(
        0, step_total, advance, (arriving_start, cache_start, finished_start)
    )
    gathered = broadcast(finished, "section", sections - 1)
    flat = gathered.reshape((GROUPS * CF, channels, height, breadth))
    return lax.dynamic_slice_in_dim(flat, my_section * share, share, 0)


def solution(mesh):
    placed = (
        P(None, None, "tile", None),
        P("section", None),
        P("section", None, None, None),
        P("section", None),
    )
    return jax.shard_map(
        on_device,
        mesh=mesh,
        in_specs=placed,
        out_specs=P("section", None, "tile", None),
        check_vma=False,
    )
```

profile of v0, /device:TPU:7, one launch (start us, length us, event | category | flops | bytes accessed | tf_op | source)
XLA Modules:
  0.0 547.4 jit_solution(3645360676454922043)
XLA Ops:
  6.5 5.3 copy.6
  11.9 4.3 copy.7
  16.2 2.0 broadcast.42
  18.3 405.7 %while.19 = (s32[]{:T(128)}, bf16[4,192,3,128]{3,1,2,0:T(8,128)(2,1)S(1)}, bf16[2,192,3,128]{3,1,2,0:T(8,128)(2,1)S(1)}, bf16[4,4,192,3,128]{4,2,3,1,0:T(8,128)(...) while((s32[]{:T(128)}, ...), condition=%wide.region_4.5_spmd.clone, body=%wide.region_0.4_spmd.clone.sunk | while | flops 3066054144 | bytes 91744152 | solution.py:118
  20.2 2.6 collective-permute-start
  22.8 5.1 collective-permute-start.1
  31.7 10.7 %conditional.3 = (f32[4,192,3,128]{3,1,2,0:T(8,128)S(1)}) conditional(s32[]{:T(128)} %convert_element_type.75, () %tuple.64, (bf16[6,192,5,128]{3,1,2,0:T(8,128)(2,1)S(1)}, bf16[3,192,1728]{2,1,0:T(8,128)(2,1)}) %tuple.65), branch_computations={%region_2.2_spmd, %region_3.3_spmd} | conditional | flops 3058237440 | bytes 73728040 | solution.py:101
  45.0 12.8 %collective-permute-done.2 = bf16[4,192,3,128]{3,1,2,0:T(8,128)(2,1)S(1)} collective-permute-done((bf16[4,192,3,128]{3,1,2,0:T(8,128)(2,1)S(1)}, bf16[4,192,3,128]{3,1,2,0:T(8,128)(2,1)S(1)}, u32[]{:S(2)}, u32[]{:S(2)}) %collective-permute-start.2) | collective-permute-done | bytes 589856 | tf_op jit(solution)/shard_map/while/body/eval_jaxpr/ppermute | solution.py:30
  59.7 2.0 collective-permute-start
  61.8 5.6 %collective-permute-start.1 = (bf16[6,192,1,128]{3,1,2,0:T(8,128)(2,1)S(1)}, bf16[6,192,1,128]{3,1,2,0:T(8,128)(2,1)S(1)}, u32[]{:S(2)}, u32[]{:S(2)}) collective-permute-start(bf16[6,192,1,128]{3,1,2,0:T(8,128)(2,1)S(1)} %get-tuple-element.383), channel_id=1, source_target_pairs={{0,1},{1,2},{2,3},{3,4},{4,5},{5,6},{6,7},{7,8},{8,9},{9,10},{10,1... | collective-permute-start | bytes 884744 | tf_op jit(solution)/shard_map/while/body/eval_jaxpr/ppermute | solution.py:18
  71.2 10.7 %conditional.3 = (f32[4,192,3,128]{3,1,2,0:T(8,128)S(1)}) conditional(s32[]{:T(128)} %convert_element_type.75, () %tuple.64, (bf16[6,192,5,128]{3,1,2,0:T(8,128)(2,1)S(1)}, bf16[3,192,1728]{2,1,0:T(8,128)(2,1)}) %tuple.65), branch_computations={%region_2.2_spmd, %region_3.3_spmd} | conditional | flops 3058237440 | bytes 73728040 | solution.py:101
  83.1 3.9 collective-permute-start.2
  87.0 12.6 %collective-permute-done.2 = bf16[4,192,3,128]{3,1,2,0:T(8,128)(2,1)S(1)} collective-permute-done((bf16[4,192,3,128]{3,1,2,0:T(8,128)(2,1)S(1)}, bf16[4,192,3,128]{3,1,2,0:T(8,128)(2,1)S(1)}, u32[]{:S(2)}, u32[]{:S(2)}) %collective-permute-start.2) | collective-permute-done | bytes 589856 | tf_op jit(solution)/shard_map/while/body/eval_jaxpr/ppermute | solution.py:30
  101.5 1.9 collective-permute-start
  103.4 5.8 %collective-permute-start.1 = (bf16[6,192,1,128]{3,1,2,0:T(8,128)(2,1)S(1)}, bf16[6,192,1,128]{3,1,2,0:T(8,128)(2,1)S(1)}, u32[]{:S(2)}, u32[]{:S(2)}) collective-permute-start(bf16[6,192,1,128]{3,1,2,0:T(8,128)(2,1)S(1)} %get-tuple-element.383), channel_id=1, source_target_pairs={{0,1},{1,2},{2,3},{3,4},{4,5},{5,6},{6,7},{7,8},{8,9},{9,10},{10,1... | collective-permute-start | bytes 884744 | tf_op jit(solution)/shard_map/while/body/eval_jaxpr/ppermute | solution.py:18
  113.0 10.7 %conditional.3 = (f32[4,192,3,128]{3,1,2,0:T(8,128)S(1)}) conditional(s32[]{:T(128)} %convert_element_type.75, () %tuple.64, (bf16[6,192,5,128]{3,1,2,0:T(8,128)(2,1)S(1)}, bf16[3,192,1728]{2,1,0:T(8,128)(2,1)}) %tuple.65), branch_computations={%region_2.2_spmd, %region_3.3_spmd} | conditional | flops 3058237440 | bytes 73728040 | solution.py:101
  124.9 3.8 collective-permute-start.2
  128.8 12.4 %collective-permute-done.2 = bf16[4,192,3,128]{3,1,2,0:T(8,128)(2,1)S(1)} collective-permute-done((bf16[4,192,3,128]{3,1,2,0:T(8,128)(2,1)S(1)}, bf16[4,192,3,128]{3,1,2,0:T(8,128)(2,1)S(1)}, u32[]{:S(2)}, u32[]{:S(2)}) %collective-permute-start.2) | collective-permute-done | bytes 589856 | tf_op jit(solution)/shard_map/while/body/eval_jaxpr/ppermute | solution.py:30
  143.1 1.9 collective-permute-start
  145.0 5.8 %collective-permute-start.1 = (bf16[6,192,1,128]{3,1,2,0:T(8,128)(2,1)S(1)}, bf16[6,192,1,128]{3,1,2,0:T(8,128)(2,1)S(1)}, u32[]{:S(2)}, u32[]{:S(2)}) collective-permute-start(bf16[6,192,1,128]{3,1,2,0:T(8,128)(2,1)S(1)} %get-tuple-element.383), channel_id=1, source_target_pairs={{0,1},{1,2},{2,3},{3,4},{4,5},{5,6},{6,7},{7,8},{8,9},{9,10},{10,1... | collective-permute-start | bytes 884744 | tf_op jit(solution)/shard_map/while/body/eval_jaxpr/ppermute | solution.py:18
  154.6 10.7 %conditional.3 = (f32[4,192,3,128]{3,1,2,0:T(8,128)S(1)}) conditional(s32[]{:T(128)} %convert_element_type.75, () %tuple.64, (bf16[6,192,5,128]{3,1,2,0:T(8,128)(2,1)S(1)}, bf16[3,192,1728]{2,1,0:T(8,128)(2,1)}) %tuple.65), branch_computations={%region_2.2_spmd, %region_3.3_spmd} | conditional | flops 3058237440 | bytes 73728040 | solution.py:101
  166.6 3.8 collective-permute-start.2
  170.4 12.3 %collective-permute-done.2 = bf16[4,192,3,128]{3,1,2,0:T(8,128)(2,1)S(1)} collective-permute-done((bf16[4,192,3,128]{3,1,2,0:T(8,128)(2,1)S(1)}, bf16[4,192,3,128]{3,1,2,0:T(8,128)(2,1)S(1)}, u32[]{:S(2)}, u32[]{:S(2)}) %collective-permute-start.2) | collective-permute-done | bytes 589856 | tf_op jit(solution)/shard_map/while/body/eval_jaxpr/ppermute | solution.py:30
  184.6 1.9 collective-permute-start
  186.5 5.8 %collective-permute-start.1 = (bf16[6,192,1,128]{3,1,2,0:T(8,128)(2,1)S(1)}, bf16[6,192,1,128]{3,1,2,0:T(8,128)(2,1)S(1)}, u32[]{:S(2)}, u32[]{:S(2)}) collective-permute-start(bf16[6,192,1,128]{3,1,2,0:T(8,128)(2,1)S(1)} %get-tuple-element.383), channel_id=1, source_target_pairs={{0,1},{1,2},{2,3},{3,4},{4,5},{5,6},{6,7},{7,8},{8,9},{9,10},{10,1... | collective-permute-start | bytes 884744 | tf_op jit(solution)/shard_map/while/body/eval_jaxpr/ppermute | solution.py:18
  197.5 14.4 %collective-permute-start.2 = (bf16[4,192,3,128]{3,1,2,0:T(8,128)(2,1)S(1)}, bf16[4,192,3,128]{3,1,2,0:T(8,128)(2,1)S(1)}, u32[]{:S(2)}, u32[]{:S(2)}) collective-permute-start(bf16[4,192,3,128]{3,1,2,0:T(8,128)(2,1)S(1)} %get-tuple-element.384), channel_id=1, source_target_pairs={{0,32},{32,64},{64,96},{96,128},{128,160},{160,192},{192,224},{1,3... | collective-permute-start | bytes 1769480 | tf_op jit(solution)/shard_map/while/body/eval_jaxpr/ppermute | solution.py:30
  211.8 12.1 %collective-permute-done.2 = bf16[4,192,3,128]{3,1,2,0:T(8,128)(2,1)S(1)} collective-permute-done((bf16[4,192,3,128]{3,1,2,0:T(8,128)(2,1)S(1)}, bf16[4,192,3,128]{3,1,2,0:T(8,128)(2,1)S(1)}, u32[]{:S(2)}, u32[]{:S(2)}) %collective-permute-start.2) | collective-permute-done | bytes 589856 | tf_op jit(solution)/shard_map/while/body/eval_jaxpr/ppermute | solution.py:30
  225.8 1.9 collective-permute-start
  227.8 5.8 %collective-permute-start.1 = (bf16[6,192,1,128]{3,1,2,0:T(8,128)(2,1)S(1)}, bf16[6,192,1,128]{3,1,2,0:T(8,128)(2,1)S(1)}, u32[]{:S(2)}, u32[]{:S(2)}) collective-permute-start(bf16[6,192,1,128]{3,1,2,0:T(8,128)(2,1)S(1)} %get-tuple-element.383), channel_id=1, source_target_pairs={{0,1},{1,2},{2,3},{3,4},{4,5},{5,6},{6,7},{7,8},{8,9},{9,10},{10,1... | collective-permute-start | bytes 884744 | tf_op jit(solution)/shard_map/while/body/eval_jaxpr/ppermute | solution.py:18
  238.7 3.8 collective-permute-start.2
  242.6 11.9 %collective-permute-done.2 = bf16[4,192,3,128]{3,1,2,0:T(8,128)(2,1)S(1)} collective-permute-done((bf16[4,192,3,128]{3,1,2,0:T(8,128)(2,1)S(1)}, bf16[4,192,3,128]{3,1,2,0:T(8,128)(2,1)S(1)}, u32[]{:S(2)}, u32[]{:S(2)}) %collective-permute-start.2) | collective-permute-done | bytes 589856 | tf_op jit(solution)/shard_map/while/body/eval_jaxpr/ppermute | solution.py:30
  258.3 5.8 %collective-permute-start.1 = (bf16[6,192,1,128]{3,1,2,0:T(8,128)(2,1)S(1)}, bf16[6,192,1,128]{3,1,2,0:T(8,128)(2,1)S(1)}, u32[]{:S(2)}, u32[]{:S(2)}) collective-permute-start(bf16[6,192,1,128]{3,1,2,0:T(8,128)(2,1)S(1)} %get-tuple-element.383), channel_id=1, source_target_pairs={{0,1},{1,2},{2,3},{3,4},{4,5},{5,6},{6,7},{7,8},{8,9},{9,10},{10,1... | collective-permute-start | bytes 884744 | tf_op jit(solution)/shard_map/while/body/eval_jaxpr/ppermute | solution.py:18
  269.2 11.9 %collective-permute-start.2 = (bf16[4,192,3,128]{3,1,2,0:T(8,128)(2,1)S(1)}, bf16[4,192,3,128]{3,1,2,0:T(8,128)(2,1)S(1)}, u32[]{:S(2)}, u32[]{:S(2)}) collective-permute-start(bf16[4,192,3,128]{3,1,2,0:T(8,128)(2,1)S(1)} %get-tuple-element.384), channel_id=1, source_target_pairs={{0,32},{32,64},{64,96},{96,128},{128,160},{160,192},{192,224},{1,3... | collective-permute-start | bytes 1769480 | tf_op jit(solution)/shard_map/while/body/eval_jaxpr/ppermute | solution.py:30
  281.1 11.0 %collective-permute-done.2 = bf16[4,192,3,128]{3,1,2,0:T(8,128)(2,1)S(1)} collective-permute-done((bf16[4,192,3,128]{3,1,2,0:T(8,128)(2,1)S(1)}, bf16[4,192,3,128]{3,1,2,0:T(8,128)(2,1)S(1)}, u32[]{:S(2)}, u32[]{:S(2)}) %collective-permute-start.2) | collective-permute-done | bytes 589856 | tf_op jit(solution)/shard_map/while/body/eval_jaxpr/ppermute | solution.py:30
  294.0 1.9 collective-permute-start
  295.9 5.8 %collective-permute-start.1 = (bf16[6,192,1,128]{3,1,2,0:T(8,128)(2,1)S(1)}, bf16[6,192,1,128]{3,1,2,0:T(8,128)(2,1)S(1)}, u32[]{:S(2)}, u32[]{:S(2)}) collective-permute-start(bf16[6,192,1,128]{3,1,2,0:T(8,128)(2,1)S(1)} %get-tuple-element.383), channel_id=1, source_target_pairs={{0,1},{1,2},{2,3},{3,4},{4,5},{5,6},{6,7},{7,8},{8,9},{9,10},{10,1... | collective-permute-start | bytes 884744 | tf_op jit(solution)/shard_map/while/body/eval_jaxpr/ppermute | solution.py:18
  306.9 4.1 collective-permute-start.2
  311.0 10.7 %collective-permute-done.2 = bf16[4,192,3,128]{3,1,2,0:T(8,128)(2,1)S(1)} collective-permute-done((bf16[4,192,3,128]{3,1,2,0:T(8,128)(2,1)S(1)}, bf16[4,192,3,128]{3,1,2,0:T(8,128)(2,1)S(1)}, u32[]{:S(2)}, u32[]{:S(2)}) %collective-permute-start.2) | collective-permute-done | bytes 589856 | tf_op jit(solution)/shard_map/while/body/eval_jaxpr/ppermute | solution.py:30
  325.6 5.8 %collective-permute-start.1 = (bf16[6,192,1,128]{3,1,2,0:T(8,128)(2,1)S(1)}, bf16[6,192,1,128]{3,1,2,0:T(8,128)(2,1)S(1)}, u32[]{:S(2)}, u32[]{:S(2)}) collective-permute-start(bf16[6,192,1,128]{3,1,2,0:T(8,128)(2,1)S(1)} %get-tuple-element.383), channel_id=1, source_target_pairs={{0,1},{1,2},{2,3},{3,4},{4,5},{5,6},{6,7},{7,8},{8,9},{9,10},{10,1... | collective-permute-start | bytes 884744 | tf_op jit(solution)/shard_map/while/body/eval_jaxpr/ppermute | solution.py:18
  336.5 11.6 %collective-permute-start.2 = (bf16[4,192,3,128]{3,1,2,0:T(8,128)(2,1)S(1)}, bf16[4,192,3,128]{3,1,2,0:T(8,128)(2,1)S(1)}, u32[]{:S(2)}, u32[]{:S(2)}) collective-permute-start(bf16[4,192,3,128]{3,1,2,0:T(8,128)(2,1)S(1)} %get-tuple-element.384), channel_id=1, source_target_pairs={{0,32},{32,64},{64,96},{96,128},{128,160},{160,192},{192,224},{1,3... | collective-permute-start | bytes 1769480 | tf_op jit(solution)/shard_map/while/body/eval_jaxpr/ppermute | solution.py:30
  348.2 9.8 %collective-permute-done.2 = bf16[4,192,3,128]{3,1,2,0:T(8,128)(2,1)S(1)} collective-permute-done((bf16[4,192,3,128]{3,1,2,0:T(8,128)(2,1)S(1)}, bf16[4,192,3,128]{3,1,2,0:T(8,128)(2,1)S(1)}, u32[]{:S(2)}, u32[]{:S(2)}) %collective-permute-start.2) | collective-permute-done | bytes 589856 | tf_op jit(solution)/shard_map/while/body/eval_jaxpr/ppermute | solution.py:30
  361.9 5.8 %collective-permute-start.1 = (bf16[6,192,1,128]{3,1,2,0:T(8,128)(2,1)S(1)}, bf16[6,192,1,128]{3,1,2,0:T(8,128)(2,1)S(1)}, u32[]{:S(2)}, u32[]{:S(2)}) collective-permute-start(bf16[6,192,1,128]{3,1,2,0:T(8,128)(2,1)S(1)} %get-tuple-element.383), channel_id=1, source_target_pairs={{0,1},{1,2},{2,3},{3,4},{4,5},{5,6},{6,7},{7,8},{8,9},{9,10},{10,1... | collective-permute-start | bytes 884744 | tf_op jit(solution)/shard_map/while/body/eval_jaxpr/ppermute | solution.py:18
  372.8 4.4 collective-permute-start.2
  377.3 9.6 %collective-permute-done.2 = bf16[4,192,3,128]{3,1,2,0:T(8,128)(2,1)S(1)} collective-permute-done((bf16[4,192,3,128]{3,1,2,0:T(8,128)(2,1)S(1)}, bf16[4,192,3,128]{3,1,2,0:T(8,128)(2,1)S(1)}, u32[]{:S(2)}, u32[]{:S(2)}) %collective-permute-start.2) | collective-permute-done | bytes 589856 | tf_op jit(solution)/shard_map/while/body/eval_jaxpr/ppermute | solution.py:30
  390.7 5.8 %collective-permute-start.1 = (bf16[6,192,1,128]{3,1,2,0:T(8,128)(2,1)S(1)}, bf16[6,192,1,128]{3,1,2,0:T(8,128)(2,1)S(1)}, u32[]{:S(2)}, u32[]{:S(2)}) collective-permute-start(bf16[6,192,1,128]{3,1,2,0:T(8,128)(2,1)S(1)} %get-tuple-element.383), channel_id=1, source_target_pairs={{0,1},{1,2},{2,3},{3,4},{4,5},{5,6},{6,7},{7,8},{8,9},{9,10},{10,1... | collective-permute-start | bytes 884744 | tf_op jit(solution)/shard_map/while/body/eval_jaxpr/ppermute | solution.py:18
  401.7 12.6 %collective-permute-start.2 = (bf16[4,192,3,128]{3,1,2,0:T(8,128)(2,1)S(1)}, bf16[4,192,3,128]{3,1,2,0:T(8,128)(2,1)S(1)}, u32[]{:S(2)}, u32[]{:S(2)}) collective-permute-start(bf16[4,192,3,128]{3,1,2,0:T(8,128)(2,1)S(1)} %get-tuple-element.384), channel_id=1, source_target_pairs={{0,32},{32,64},{64,96},{96,128},{128,160},{160,192},{192,224},{1,3... | collective-permute-start | bytes 1769480 | tf_op jit(solution)/shard_map/while/body/eval_jaxpr/ppermute | solution.py:30
  414.3 9.6 %collective-permute-done.2 = bf16[4,192,3,128]{3,1,2,0:T(8,128)(2,1)S(1)} collective-permute-done((bf16[4,192,3,128]{3,1,2,0:T(8,128)(2,1)S(1)}, bf16[4,192,3,128]{3,1,2,0:T(8,128)(2,1)S(1)}, u32[]{:S(2)}, u32[]{:S(2)}) %collective-permute-start.2) | collective-permute-done | bytes 589856 | tf_op jit(solution)/shard_map/while/body/eval_jaxpr/ppermute | solution.py:30
  425.6 113.3 %all-reduce.3.cloned.1.call-done = bf16[16,192,3,128]{3,1,2,0:T(8,128)(2,1)} async-done(((bf16[16,192,3,128]{3,1,2,0:T(8,128)(2,1)}), bf16[16,192,3,128]{3,1,2,0:T(8,128)(2,1)}) %all-reduce.3.cloned.1.call-update) | async-done | bytes 2359312 | tf_op jit(solution)/shard_map/psum | solution.py:35
  (247 shorter events, 131.9 us)
Async XLA Ops:
  6.5 532.3 %all-reduce.3.cloned.1.call-start = ((), (), s32[]{:S(2)}) async-start(), calls=%async_computation | async-start | bytes 4718592 | tf_op jit(solution)/shard_map/psum | solution.py:35
  11.9 6.4 %copy-start.1 = (f32[1,192]{1,0:T(1,128)S(1)}, f32[1,192]{1,0:T(1,128)}, u32[]{:S(2)}) copy-start(f32[1,192]{1,0:T(1,128)} %param.11) | copy-start | bytes 2308
  11.9 6.4 %copy-start.2 = (f32[1,192]{1,0:T(1,128)S(1)}, f32[1,192]{1,0:T(1,128)}, u32[]{:S(2)}) copy-start(f32[1,192]{1,0:T(1,128)} %param.9) | copy-start | bytes 2308
  20.2 10.2 %collective-permute-start = (bf16[6,192,1,128]{3,1,2,0:T(8,128)(2,1)S(1)}, bf16[6,192,1,128]{3,1,2,0:T(8,128)(2,1)S(1)}, u32[]{:S(2)}, u32[]{:S(2)}) collective-permute-start(bf16[6,192,1,128]{3,1,2,0:T(8,128)(2,1)S(1)} %get-tuple-element.382), channel_id=1, source_target_pairs={{1,0},{2,1},{3,2},{4,3},{5,4},{6,5},{7,6},{8,7},{9,8},{10,9},{11,1... | collective-permute-start | bytes 884744 | tf_op jit(solution)/shard_map/while/body/eval_jaxpr/ppermute | solution.py:20
  22.8 8.7 %collective-permute-start.1 = (bf16[6,192,1,128]{3,1,2,0:T(8,128)(2,1)S(1)}, bf16[6,192,1,128]{3,1,2,0:T(8,128)(2,1)S(1)}, u32[]{:S(2)}, u32[]{:S(2)}) collective-permute-start(bf16[6,192,1,128]{3,1,2,0:T(8,128)(2,1)S(1)} %get-tuple-element.383), channel_id=1, source_target_pairs={{0,1},{1,2},{2,3},{3,4},{4,5},{5,6},{6,7},{7,8},{8,9},{9,10},{10,1... | collective-permute-start | bytes 884744 | tf_op jit(solution)/shard_map/while/body/eval_jaxpr/ppermute | solution.py:18
  37.1 1.6 copy-start
  43.6 14.2 %collective-permute-start.2 = (bf16[4,192,3,128]{3,1,2,0:T(8,128)(2,1)S(1)}, bf16[4,192,3,128]{3,1,2,0:T(8,128)(2,1)S(1)}, u32[]{:S(2)}, u32[]{:S(2)}) collective-permute-start(bf16[4,192,3,128]{3,1,2,0:T(8,128)(2,1)S(1)} %get-tuple-element.384), channel_id=1, source_target_pairs={{0,32},{32,64},{64,96},{96,128},{128,160},{160,192},{192,224},{1,3... | collective-permute-start | bytes 1769480 | tf_op jit(solution)/shard_map/while/body/eval_jaxpr/ppermute | solution.py:30
  59.7 10.2 %collective-permute-start = (bf16[6,192,1,128]{3,1,2,0:T(8,128)(2,1)S(1)}, bf16[6,192,1,128]{3,1,2,0:T(8,128)(2,1)S(1)}, u32[]{:S(2)}, u32[]{:S(2)}) collective-permute-start(bf16[6,192,1,128]{3,1,2,0:T(8,128)(2,1)S(1)} %get-tuple-element.382), channel_id=1, source_target_pairs={{1,0},{2,1},{3,2},{4,3},{5,4},{6,5},{7,6},{8,7},{9,8},{10,9},{11,1... | collective-permute-start | bytes 884744 | tf_op jit(solution)/shard_map/while/body/eval_jaxpr/ppermute | solution.py:20
  61.8 9.3 %collective-permute-start.1 = (bf16[6,192,1,128]{3,1,2,0:T(8,128)(2,1)S(1)}, bf16[6,192,1,128]{3,1,2,0:T(8,128)(2,1)S(1)}, u32[]{:S(2)}, u32[]{:S(2)}) collective-permute-start(bf16[6,192,1,128]{3,1,2,0:T(8,128)(2,1)S(1)} %get-tuple-element.383), channel_id=1, source_target_pairs={{0,1},{1,2},{2,3},{3,4},{4,5},{5,6},{6,7},{7,8},{8,9},{9,10},{10,1... | collective-permute-start | bytes 884744 | tf_op jit(solution)/shard_map/while/body/eval_jaxpr/ppermute | solution.py:18
  76.6 1.6 copy-start
  83.1 16.5 %collective-permute-start.2 = (bf16[4,192,3,128]{3,1,2,0:T(8,128)(2,1)S(1)}, bf16[4,192,3,128]{3,1,2,0:T(8,128)(2,1)S(1)}, u32[]{:S(2)}, u32[]{:S(2)}) collective-permute-start(bf16[4,192,3,128]{3,1,2,0:T(8,128)(2,1)S(1)} %get-tuple-element.384), channel_id=1, source_target_pairs={{0,32},{32,64},{64,96},{96,128},{128,160},{160,192},{192,224},{1,3... | collective-permute-start | bytes 1769480 | tf_op jit(solution)/shard_map/while/body/eval_jaxpr/ppermute | solution.py:30
  101.5 10.2 %collective-permute-start = (bf16[6,192,1,128]{3,1,2,0:T(8,128)(2,1)S(1)}, bf16[6,192,1,128]{3,1,2,0:T(8,128)(2,1)S(1)}, u32[]{:S(2)}, u32[]{:S(2)}) collective-permute-start(bf16[6,192,1,128]{3,1,2,0:T(8,128)(2,1)S(1)} %get-tuple-element.382), channel_id=1, source_target_pairs={{1,0},{2,1},{3,2},{4,3},{5,4},{6,5},{7,6},{8,7},{9,8},{10,9},{11,1... | collective-permute-start | bytes 884744 | tf_op jit(solution)/shard_map/while/body/eval_jaxpr/ppermute | solution.py:20
  103.4 9.4 %collective-permute-start.1 = (bf16[6,192,1,128]{3,1,2,0:T(8,128)(2,1)S(1)}, bf16[6,192,1,128]{3,1,2,0:T(8,128)(2,1)S(1)}, u32[]{:S(2)}, u32[]{:S(2)}) collective-permute-start(bf16[6,192,1,128]{3,1,2,0:T(8,128)(2,1)S(1)} %get-tuple-element.383), channel_id=1, source_target_pairs={{0,1},{1,2},{2,3},{3,4},{4,5},{5,6},{6,7},{7,8},{8,9},{9,10},{10,1... | collective-permute-start | bytes 884744 | tf_op jit(solution)/shard_map/while/body/eval_jaxpr/ppermute | solution.py:18
  118.4 1.6 copy-start
  124.9 16.3 %collective-permute-start.2 = (bf16[4,192,3,128]{3,1,2,0:T(8,128)(2,1)S(1)}, bf16[4,192,3,128]{3,1,2,0:T(8,128)(2,1)S(1)}, u32[]{:S(2)}, u32[]{:S(2)}) collective-permute-start(bf16[4,192,3,128]{3,1,2,0:T(8,128)(2,1)S(1)} %get-tuple-element.384), channel_id=1, source_target_pairs={{0,32},{32,64},{64,96},{96,128},{128,160},{160,192},{192,224},{1,3... | collective-permute-start | bytes 1769480 | tf_op jit(solution)/shard_map/while/body/eval_jaxpr/ppermute | solution.py:30
  143.1 10.2 %collective-permute-start = (bf16[6,192,1,128]{3,1,2,0:T(8,128)(2,1)S(1)}, bf16[6,192,1,128]{3,1,2,0:T(8,128)(2,1)S(1)}, u32[]{:S(2)}, u32[]{:S(2)}) collective-permute-start(bf16[6,192,1,128]{3,1,2,0:T(8,128)(2,1)S(1)} %get-tuple-element.382), channel_id=1, source_target_pairs={{1,0},{2,1},{3,2},{4,3},{5,4},{6,5},{7,6},{8,7},{9,8},{10,9},{11,1... | collective-permute-start | bytes 884744 | tf_op jit(solution)/shard_map/while/body/eval_jaxpr/ppermute | solution.py:20
  145.0 9.4 %collective-permute-start.1 = (bf16[6,192,1,128]{3,1,2,0:T(8,128)(2,1)S(1)}, bf16[6,192,1,128]{3,1,2,0:T(8,128)(2,1)S(1)}, u32[]{:S(2)}, u32[]{:S(2)}) collective-permute-start(bf16[6,192,1,128]{3,1,2,0:T(8,128)(2,1)S(1)} %get-tuple-element.383), channel_id=1, source_target_pairs={{0,1},{1,2},{2,3},{3,4},{4,5},{5,6},{6,7},{7,8},{8,9},{9,10},{10,1... | collective-permute-start | bytes 884744 | tf_op jit(solution)/shard_map/while/body/eval_jaxpr/ppermute | solution.py:18
  160.0 1.6 copy-start
  166.6 16.1 %collective-permute-start.2 = (bf16[4,192,3,128]{3,1,2,0:T(8,128)(2,1)S(1)}, bf16[4,192,3,128]{3,1,2,0:T(8,128)(2,1)S(1)}, u32[]{:S(2)}, u32[]{:S(2)}) collective-permute-start(bf16[4,192,3,128]{3,1,2,0:T(8,128)(2,1)S(1)} %get-tuple-element.384), channel_id=1, source_target_pairs={{0,32},{32,64},{64,96},{96,128},{128,160},{160,192},{192,224},{1,3... | collective-permute-start | bytes 1769480 | tf_op jit(solution)/shard_map/while/body/eval_jaxpr/ppermute | solution.py:30
  184.6 10.2 %collective-permute-start = (bf16[6,192,1,128]{3,1,2,0:T(8,128)(2,1)S(1)}, bf16[6,192,1,128]{3,1,2,0:T(8,128)(2,1)S(1)}, u32[]{:S(2)}, u32[]{:S(2)}) collective-permute-start(bf16[6,192,1,128]{3,1,2,0:T(8,128)(2,1)S(1)} %get-tuple-element.382), channel_id=1, source_target_pairs={{1,0},{2,1},{3,2},{4,3},{5,4},{6,5},{7,6},{8,7},{9,8},{10,9},{11,1... | collective-permute-start | bytes 884744 | tf_op jit(solution)/shard_map/while/body/eval_jaxpr/ppermute | solution.py:20
  186.5 9.4 %collective-permute-start.1 = (bf16[6,192,1,128]{3,1,2,0:T(8,128)(2,1)S(1)}, bf16[6,192,1,128]{3,1,2,0:T(8,128)(2,1)S(1)}, u32[]{:S(2)}, u32[]{:S(2)}) collective-permute-start(bf16[6,192,1,128]{3,1,2,0:T(8,128)(2,1)S(1)} %get-tuple-element.383), channel_id=1, source_target_pairs={{0,1},{1,2},{2,3},{3,4},{4,5},{5,6},{6,7},{7,8},{8,9},{9,10},{10,1... | collective-permute-start | bytes 884744 | tf_op jit(solution)/shard_map/while/body/eval_jaxpr/ppermute | solution.py:18
  197.5 26.5 %collective-permute-start.2 = (bf16[4,192,3,128]{3,1,2,0:T(8,128)(2,1)S(1)}, bf16[4,192,3,128]{3,1,2,0:T(8,128)(2,1)S(1)}, u32[]{:S(2)}, u32[]{:S(2)}) collective-permute-start(bf16[4,192,3,128]{3,1,2,0:T(8,128)(2,1)S(1)} %get-tuple-element.384), channel_id=1, source_target_pairs={{0,32},{32,64},{64,96},{96,128},{128,160},{160,192},{192,224},{1,3... | collective-permute-start | bytes 1769480 | tf_op jit(solution)/shard_map/while/body/eval_jaxpr/ppermute | solution.py:30
  225.8 10.2 %collective-permute-start = (bf16[6,192,1,128]{3,1,2,0:T(8,128)(2,1)S(1)}, bf16[6,192,1,128]{3,1,2,0:T(8,128)(2,1)S(1)}, u32[]{:S(2)}, u32[]{:S(2)}) collective-permute-start(bf16[6,192,1,128]{3,1,2,0:T(8,128)(2,1)S(1)} %get-tuple-element.382), channel_id=1, source_target_pairs={{1,0},{2,1},{3,2},{4,3},{5,4},{6,5},{7,6},{8,7},{9,8},{10,9},{11,1... | collective-permute-start | bytes 884744 | tf_op jit(solution)/shard_map/while/body/eval_jaxpr/ppermute | solution.py:20
  227.8 9.4 %collective-permute-start.1 = (bf16[6,192,1,128]{3,1,2,0:T(8,128)(2,1)S(1)}, bf16[6,192,1,128]{3,1,2,0:T(8,128)(2,1)S(1)}, u32[]{:S(2)}, u32[]{:S(2)}) collective-permute-start(bf16[6,192,1,128]{3,1,2,0:T(8,128)(2,1)S(1)} %get-tuple-element.383), channel_id=1, source_target_pairs={{0,1},{1,2},{2,3},{3,4},{4,5},{5,6},{6,7},{7,8},{8,9},{9,10},{10,1... | collective-permute-start | bytes 884744 | tf_op jit(solution)/shard_map/while/body/eval_jaxpr/ppermute | solution.py:18
  238.7 15.7 %collective-permute-start.2 = (bf16[4,192,3,128]{3,1,2,0:T(8,128)(2,1)S(1)}, bf16[4,192,3,128]{3,1,2,0:T(8,128)(2,1)S(1)}, u32[]{:S(2)}, u32[]{:S(2)}) collective-permute-start(bf16[4,192,3,128]{3,1,2,0:T(8,128)(2,1)S(1)} %get-tuple-element.384), channel_id=1, source_target_pairs={{0,32},{32,64},{64,96},{96,128},{128,160},{160,192},{192,224},{1,3... | collective-permute-start | bytes 1769480 | tf_op jit(solution)/shard_map/while/body/eval_jaxpr/ppermute | solution.py:30
  256.3 10.2 %collective-permute-start = (bf16[6,192,1,128]{3,1,2,0:T(8,128)(2,1)S(1)}, bf16[6,192,1,128]{3,1,2,0:T(8,128)(2,1)S(1)}, u32[]{:S(2)}, u32[]{:S(2)}) collective-permute-start(bf16[6,192,1,128]{3,1,2,0:T(8,128)(2,1)S(1)} %get-tuple-element.382), channel_id=1, source_target_pairs={{1,0},{2,1},{3,2},{4,3},{5,4},{6,5},{7,6},{8,7},{9,8},{10,9},{11,1... | collective-permute-start | bytes 884744 | tf_op jit(solution)/shard_map/while/body/eval_jaxpr/ppermute | solution.py:20
  258.3 9.4 %collective-permute-start.1 = (bf16[6,192,1,128]{3,1,2,0:T(8,128)(2,1)S(1)}, bf16[6,192,1,128]{3,1,2,0:T(8,128)(2,1)S(1)}, u32[]{:S(2)}, u32[]{:S(2)}) collective-permute-start(bf16[6,192,1,128]{3,1,2,0:T(8,128)(2,1)S(1)} %get-tuple-element.383), channel_id=1, source_target_pairs={{0,1},{1,2},{2,3},{3,4},{4,5},{5,6},{6,7},{7,8},{8,9},{9,10},{10,1... | collective-permute-start | bytes 884744 | tf_op jit(solution)/shard_map/while/body/eval_jaxpr/ppermute | solution.py:18
  269.2 22.9 %collective-permute-start.2 = (bf16[4,192,3,128]{3,1,2,0:T(8,128)(2,1)S(1)}, bf16[4,192,3,128]{3,1,2,0:T(8,128)(2,1)S(1)}, u32[]{:S(2)}, u32[]{:S(2)}) collective-permute-start(bf16[4,192,3,128]{3,1,2,0:T(8,128)(2,1)S(1)} %get-tuple-element.384), channel_id=1, source_target_pairs={{0,32},{32,64},{64,96},{96,128},{128,160},{160,192},{192,224},{1,3... | collective-permute-start | bytes 1769480 | tf_op jit(solution)/shard_map/while/body/eval_jaxpr/ppermute | solution.py:30
  294.0 10.2 %collective-permute-start = (bf16[6,192,1,128]{3,1,2,0:T(8,128)(2,1)S(1)}, bf16[6,192,1,128]{3,1,2,0:T(8,128)(2,1)S(1)}, u32[]{:S(2)}, u32[]{:S(2)}) collective-permute-start(bf16[6,192,1,128]{3,1,2,0:T(8,128)(2,1)S(1)} %get-tuple-element.382), channel_id=1, source_target_pairs={{1,0},{2,1},{3,2},{4,3},{5,4},{6,5},{7,6},{8,7},{9,8},{10,9},{11,1... | collective-permute-start | bytes 884744 | tf_op jit(solution)/shard_map/while/body/eval_jaxpr/ppermute | solution.py:20
  295.9 9.4 %collective-permute-start.1 = (bf16[6,192,1,128]{3,1,2,0:T(8,128)(2,1)S(1)}, bf16[6,192,1,128]{3,1,2,0:T(8,128)(2,1)S(1)}, u32[]{:S(2)}, u32[]{:S(2)}) collective-permute-start(bf16[6,192,1,128]{3,1,2,0:T(8,128)(2,1)S(1)} %get-tuple-element.383), channel_id=1, source_target_pairs={{0,1},{1,2},{2,3},{3,4},{4,5},{5,6},{6,7},{7,8},{8,9},{9,10},{10,1... | collective-permute-start | bytes 884744 | tf_op jit(solution)/shard_map/while/body/eval_jaxpr/ppermute | solution.py:18
  306.9 14.8 %collective-permute-start.2 = (bf16[4,192,3,128]{3,1,2,0:T(8,128)(2,1)S(1)}, bf16[4,192,3,128]{3,1,2,0:T(8,128)(2,1)S(1)}, u32[]{:S(2)}, u32[]{:S(2)}) collective-permute-start(bf16[4,192,3,128]{3,1,2,0:T(8,128)(2,1)S(1)} %get-tuple-element.384), channel_id=1, source_target_pairs={{0,32},{32,64},{64,96},{96,128},{128,160},{160,192},{192,224},{1,3... | collective-permute-start | bytes 1769480 | tf_op jit(solution)/shard_map/while/body/eval_jaxpr/ppermute | solution.py:30
  323.6 10.2 %collective-permute-start = (bf16[6,192,1,128]{3,1,2,0:T(8,128)(2,1)S(1)}, bf16[6,192,1,128]{3,1,2,0:T(8,128)(2,1)S(1)}, u32[]{:S(2)}, u32[]{:S(2)}) collective-permute-start(bf16[6,192,1,128]{3,1,2,0:T(8,128)(2,1)S(1)} %get-tuple-element.382), channel_id=1, source_target_pairs={{1,0},{2,1},{3,2},{4,3},{5,4},{6,5},{7,6},{8,7},{9,8},{10,9},{11,1... | collective-permute-start | bytes 884744 | tf_op jit(solution)/shard_map/while/body/eval_jaxpr/ppermute | solution.py:20
  325.6 9.4 %collective-permute-start.1 = (bf16[6,192,1,128]{3,1,2,0:T(8,128)(2,1)S(1)}, bf16[6,192,1,128]{3,1,2,0:T(8,128)(2,1)S(1)}, u32[]{:S(2)}, u32[]{:S(2)}) collective-permute-start(bf16[6,192,1,128]{3,1,2,0:T(8,128)(2,1)S(1)} %get-tuple-element.383), channel_id=1, source_target_pairs={{0,1},{1,2},{2,3},{3,4},{4,5},{5,6},{6,7},{7,8},{8,9},{9,10},{10,1... | collective-permute-start | bytes 884744 | tf_op jit(solution)/shard_map/while/body/eval_jaxpr/ppermute | solution.py:18
  336.5 21.5 %collective-permute-start.2 = (bf16[4,192,3,128]{3,1,2,0:T(8,128)(2,1)S(1)}, bf16[4,192,3,128]{3,1,2,0:T(8,128)(2,1)S(1)}, u32[]{:S(2)}, u32[]{:S(2)}) collective-permute-start(bf16[4,192,3,128]{3,1,2,0:T(8,128)(2,1)S(1)} %get-tuple-element.384), channel_id=1, source_target_pairs={{0,32},{32,64},{64,96},{96,128},{128,160},{160,192},{192,224},{1,3... | collective-permute-start | bytes 1769480 | tf_op jit(solution)/shard_map/while/body/eval_jaxpr/ppermute | solution.py:30
  359.9 10.2 %collective-permute-start = (bf16[6,192,1,128]{3,1,2,0:T(8,128)(2,1)S(1)}, bf16[6,192,1,128]{3,1,2,0:T(8,128)(2,1)S(1)}, u32[]{:S(2)}, u32[]{:S(2)}) collective-permute-start(bf16[6,192,1,128]{3,1,2,0:T(8,128)(2,1)S(1)} %get-tuple-element.382), channel_id=1, source_target_pairs={{1,0},{2,1},{3,2},{4,3},{5,4},{6,5},{7,6},{8,7},{9,8},{10,9},{11,1... | collective-permute-start | bytes 884744 | tf_op jit(solution)/shard_map/while/body/eval_jaxpr/ppermute | solution.py:20
  361.9 9.4 %collective-permute-start.1 = (bf16[6,192,1,128]{3,1,2,0:T(8,128)(2,1)S(1)}, bf16[6,192,1,128]{3,1,2,0:T(8,128)(2,1)S(1)}, u32[]{:S(2)}, u32[]{:S(2)}) collective-permute-start(bf16[6,192,1,128]{3,1,2,0:T(8,128)(2,1)S(1)} %get-tuple-element.383), channel_id=1, source_target_pairs={{0,1},{1,2},{2,3},{3,4},{4,5},{5,6},{6,7},{7,8},{8,9},{9,10},{10,1... | collective-permute-start | bytes 884744 | tf_op jit(solution)/shard_map/while/body/eval_jaxpr/ppermute | solution.py:18
  372.8 14.1 %collective-permute-start.2 = (bf16[4,192,3,128]{3,1,2,0:T(8,128)(2,1)S(1)}, bf16[4,192,3,128]{3,1,2,0:T(8,128)(2,1)S(1)}, u32[]{:S(2)}, u32[]{:S(2)}) collective-permute-start(bf16[4,192,3,128]{3,1,2,0:T(8,128)(2,1)S(1)} %get-tuple-element.384), channel_id=1, source_target_pairs={{0,32},{32,64},{64,96},{96,128},{128,160},{160,192},{192,224},{1,3... | collective-permute-start | bytes 1769480 | tf_op jit(solution)/shard_map/while/body/eval_jaxpr/ppermute | solution.py:30
  388.8 10.2 %collective-permute-start = (bf16[6,192,1,128]{3,1,2,0:T(8,128)(2,1)S(1)}, bf16[6,192,1,128]{3,1,2,0:T(8,128)(2,1)S(1)}, u32[]{:S(2)}, u32[]{:S(2)}) collective-permute-start(bf16[6,192,1,128]{3,1,2,0:T(8,128)(2,1)S(1)} %get-tuple-element.382), channel_id=1, source_target_pairs={{1,0},{2,1},{3,2},{4,3},{5,4},{6,5},{7,6},{8,7},{9,8},{10,9},{11,1... | collective-permute-start | bytes 884744 | tf_op jit(solution)/shard_map/while/body/eval_jaxpr/ppermute | solution.py:20
  390.7 9.4 %collective-permute-start.1 = (bf16[6,192,1,128]{3,1,2,0:T(8,128)(2,1)S(1)}, bf16[6,192,1,128]{3,1,2,0:T(8,128)(2,1)S(1)}, u32[]{:S(2)}, u32[]{:S(2)}) collective-permute-start(bf16[6,192,1,128]{3,1,2,0:T(8,128)(2,1)S(1)} %get-tuple-element.383), channel_id=1, source_target_pairs={{0,1},{1,2},{2,3},{3,4},{4,5},{5,6},{6,7},{7,8},{8,9},{9,10},{10,1... | collective-permute-start | bytes 884744 | tf_op jit(solution)/shard_map/while/body/eval_jaxpr/ppermute | solution.py:18
  401.7 22.3 %collective-permute-start.2 = (bf16[4,192,3,128]{3,1,2,0:T(8,128)(2,1)S(1)}, bf16[4,192,3,128]{3,1,2,0:T(8,128)(2,1)S(1)}, u32[]{:S(2)}, u32[]{:S(2)}) collective-permute-start(bf16[4,192,3,128]{3,1,2,0:T(8,128)(2,1)S(1)} %get-tuple-element.384), channel_id=1, source_target_pairs={{0,32},{32,64},{64,96},{96,128},{128,160},{160,192},{192,224},{1,3... | collective-permute-start | bytes 1769480 | tf_op jit(solution)/shard_map/while/body/eval_jaxpr/ppermute | solution.py:30
Sparse Core Ops, SparseCore 0:
  425.7 113.1 all-reduce.2
where the time goes:
time: 553 us; the launch traced here: 547 us
  waiting for transfers between devices  266 us (48%)
  starting transfers between devices  160 us (29%)
  local copies, waits for them, and re-layouts  53.2 us (10%)
  other arithmetic  37.8 us (7%)
  matrix products  14.9 us (3%)
  between operations  13.4 us (2%)
    ppermute x11, waiting for transfers between devices, shifted(): return lax.ppermute(value, axis, pairs)  125 us
    psum x1, waiting for transfers between devices, broadcast(): return lax.psum(block, axis)  113 us
    ppermute x11, starting transfers between devices, shifted(): return lax.ppermute(value, axis, pairs)  75.8 us
    ppermute x11, starting transfers between devices, padded_2(): lax.ppermute(tail, axis, [(i, (i + 1) % count) for i in range(ends)])  62.5 us
    ppermute x11, starting transfers between devices, padded_2(): lax.ppermute(head, axis, [((i + 1) % count, i) for i in range(ends)])  21.9 us
    cond x84, local copies, waits for them, and re-layouts  20.3 us
    dot_general x12, matrix products, apply_conv(): jnp.einsum('ok,tkrw->torw', weight_cat[time_off], tap_stack, preferred_el...  14.9 us
    ppermute x11, waiting for transfers between devices, padded_2(): lax.ppermute(head, axis, [((i + 1) % count, i) for i in range(ends)])  14.8 us
  transfers between devices with their start and end apart: 34, of which 34 were waited for; matrix products, arithmetic and copies ran while one was open for 2% of the time, Pallas kernels for 0%

commit v1 on v0

v1 whole, which is shorter than its diff:
```python
import functools

import jax
import jax.numpy as jnp
from jax import lax
from jax.experimental import pallas as pl
from jax.experimental.pallas import tpu as pltpu
from jax.sharding import PartitionSpec as P

LAYERS = 8
C = 192
CP = 256
T = 16
KT = 14 * 128
STRIP = 16
PIECE = 288
SMALL = 16
FIRST = 2


def tap_piece(weight, tile):
    tap = lax.dynamic_index_in_dim(weight, jnp.minimum(tile, 26), 0, keepdims=False).T
    low = tap[:, :128]
    high = jnp.concatenate([tap[: C // 2, 128:], tap[C // 2 :, 128:]], axis=1)
    return jnp.concatenate([low, high], axis=0)


def three_parts(vector):
    high = lax.reduce_precision(vector, 8, 7)
    rest = vector - high
    middle = lax.reduce_precision(rest, 8, 7)
    return jnp.stack([high, middle, rest - middle]).astype(jnp.bfloat16)


def layer_kernel(
    win, base_ref, top_ref, r0_ref, r1_ref, r2_ref, bot_ref, w_ref, gain_ref, bias_ref,
    o0_ref, o1_ref, o2_ref, x9, wbuf,
):
    wout = win - 2
    for b in range(3):
        for e in range(3):
            for a in range(3):
                tap = 9 * a + 3 * b + e
                for lo, hi, src in ((0, 96, 0), (96, 192, 1)):
                    rows = w_ref[tap, lo:hi, :]
                    high = w_ref[tap, 192:288, :].astype(jnp.float32)
                    if src:
                        high = pltpu.roll(high, 64, 1)
                    lane = lax.broadcasted_iota(jnp.int32, high.shape, 1)
                    high = jnp.where(lane < 64, high, 0.0).astype(jnp.bfloat16)
                    both = jnp.concatenate([rows, high], axis=1)
                    full = (e * 3 + a) * 128
                    if a < 2:
                        half = (9 + e) * 128 + 64 * a
                    else:
                        half = 12 * 128 + 64 * e
                    if src == 0:
                        wbuf[b, full : full + 96, :] = both
                    else:
                        wbuf[b, full + 96 : full + 128, :] = both[:32]
                        wbuf[b, half : half + 64, :] = both[32:]
        wbuf[b, KT - 64 : KT, :] = jnp.zeros((64, CP), jnp.bfloat16)

    gain = gain_ref[...].reshape(1, 1, CP)
    for row, ref in enumerate((top_ref, r0_ref, r1_ref, r2_ref, bot_ref)):

        @pl.loop(0, win, step=2)
        def _(col, row=row, ref=ref):
            v = ref[pl.ds(col, 2)].astype(jnp.float32)
            ms = jnp.sum(v * v, axis=2, keepdims=True) * (1.0 / C)
            g = v * lax.rsqrt(ms + 1e-6) * gain
            h = g / (1.0 + jnp.exp(-g))
            time = lax.broadcasted_iota(jnp.int32, h.shape, 1)
            late1 = jnp.where(time >= 1, pltpu.roll(h, 1, 1), 0.0)
            late2 = jnp.where(time >= 2, pltpu.roll(h, 2, 1), 0.0)
            by_tap = [late2, late1, h]
            low = [p[:, :, :128].astype(jnp.bfloat16) for p in by_tap]
            pair = (late2[:, :, 128:] + pltpu.roll(late1[:, :, 128:], 64, 2)).astype(
                jnp.bfloat16
            )
            last = h[:, :, 128:].astype(jnp.bfloat16)
            moved = pltpu.roll(h[:, :, 128:], 64, 2).astype(jnp.bfloat16)
            for e in range(3):
                at = pl.ds(col + 2 - e, 2)
                for a in range(3):
                    tile = e * 3 + a
                    x9[row, at, :, tile * 128 : (tile + 1) * 128] = low[a]
                x9[row, at, :, (9 + e) * 128 : (10 + e) * 128] = pair
            x9[row, pl.ds(col + 2, 2), :, 12 * 128 : 13 * 128] = last
            before = x9[row, pl.ds(col + 1, 2), :, 12 * 128 : 13 * 128]
            lane = lax.broadcasted_iota(jnp.int32, before.shape, 2)
            x9[row, pl.ds(col + 1, 2), :, 12 * 128 : 13 * 128] = jnp.where(
                lane < 64, before, moved
            )
            x9[row, pl.ds(col, 2), :, 13 * 128 : 14 * 128] = last

    bias = bias_ref[...].reshape(1, 1, CP)
    for row, (src, out) in enumerate(((r0_ref, o0_ref), (r1_ref, o1_ref), (r2_ref, o2_ref))):
        acc = jnp.zeros((wout * T, CP), jnp.float32)
        for b in range(3):
            left = x9[row + b, 2 : 2 + wout].reshape(wout * T, KT)
            acc = acc + jnp.dot(left, wbuf[b], preferred_element_type=jnp.float32)
        new = src[1 : 1 + wout].astype(jnp.float32) + acc.reshape(wout, T, CP) + bias
        where = base_ref[0] + 1 + lax.broadcasted_iota(jnp.int32, new.shape, 0)
        inside = jnp.logical_and(where >= 0, where < 128)
        out[...] = jnp.where(inside, new, 0.0).astype(jnp.bfloat16)


def run_layer(win, which, base, top, rows, bot, weights, gain, bias):
    wout = win - 2
    whole = pl.BlockSpec(memory_space=pltpu.VMEM)
    row_shape = jax.ShapeDtypeStruct((wout, T, CP), jnp.bfloat16)
    return pl.pallas_call(
        functools.partial(layer_kernel, win),
        grid=(1,),
        out_shape=[row_shape] * 3,
        in_specs=[pl.BlockSpec(memory_space=pltpu.SMEM)]
        + [pl.BlockSpec((win, T, CP), lambda i: (0, 0, 0))] * 5
        + [pl.BlockSpec((32, None, PIECE, 128), lambda i: (0, which, 0, 0))]
        + [pl.BlockSpec((1, CP), lambda i: (0, 0))] * 2,
        out_specs=[pl.BlockSpec((wout, T, CP), lambda i: (0, 0, 0))] * 3,
        scratch_shapes=[
            pltpu.VMEM((5, win + 2, T, KT), jnp.bfloat16),
            pltpu.VMEM((3, KT, CP), jnp.bfloat16),
        ],
        compiler_params=pltpu.CompilerParams(vmem_limit_bytes=40 * 1024 * 1024),
        cost_estimate=pl.CostEstimate(
            flops=2 * 3 * wout * T * 9 * 3 * C * C, bytes_accessed=4 << 20, transcendentals=0
        ),
    )(base, top, *rows, bot, weights, gain, bias)


def on_device(frames_in, norm_gain, conv_weight, conv_bias):
    section = lax.axis_index("section")
    tile = lax.axis_index("tile")
    tiles = lax.axis_size("tile")

    small = jnp.concatenate(
        [three_parts(norm_gain[0]).reshape(-1), three_parts(conv_bias[0]).reshape(-1)]
    )
    small = jnp.pad(small, (0, SMALL * 128 - small.shape[0])).reshape(SMALL, 128)
    piece = jnp.concatenate([tap_piece(conv_weight[0], tile), small], axis=0)
    rel = [piece]
    for k in range(1, LAYERS):
        rel.append(
            lax.ppermute(piece, "section", [(i, (i + k) % LAYERS) for i in range(LAYERS)])
        )
    rel = jnp.stack(rel)
    order = jnp.mod(section - jnp.arange(LAYERS), LAYERS)
    pieces = jnp.take(rel, order, axis=0)
    parts = (
        pieces[:, PIECE:].astype(jnp.float32).reshape(LAYERS, SMALL * 128)[:, : 6 * C]
    ).reshape(LAYERS, 2, 3, C)
    vectors = parts[:, :, 0] + parts[:, :, 1] + parts[:, :, 2]
    vectors = jnp.pad(vectors, ((0, 0), (0, 0), (0, CP - C)))
    early = lax.all_gather(pieces[:FIRST, :PIECE], "tile")
    late = lax.all_gather(pieces[FIRST:, :PIECE], "tile")

    padded = jnp.pad(frames_in, ((0, 0), (0, 0), (0, 0), (LAYERS, LAYERS)))
    strip = lax.dynamic_slice_in_dim(padded, section * STRIP, STRIP + 2 * LAYERS, axis=3)
    strip = jnp.pad(strip.transpose(2, 3, 0, 1), ((0, 0), (0, 0), (0, 0), (0, CP - C)))
    rows = [strip[0], strip[1], strip[2]]
    down = [(i, i + 1) for i in range(tiles - 1)]
    up = [(i + 1, i) for i in range(tiles - 1)]
    for layer in range(LAYERS):
        win = STRIP + 2 * (LAYERS - layer)
        top = lax.ppermute(rows[2], "tile", down)
        bot = lax.ppermute(rows[0], "tile", up)
        base = (section * STRIP - (LAYERS - layer)).astype(jnp.int32).reshape(1)
        weights, which = (early, layer) if layer < FIRST else (late, layer - FIRST)
        rows = run_layer(
            win, which, base, top, rows, bot, weights,
            vectors[layer, 0:1], vectors[layer, 1:2],
        )

    share = T // LAYERS
    out = jnp.stack([row[:, :, :C] for row in rows])
    out = out.transpose(2, 0, 1, 3).reshape(LAYERS, share, 3, STRIP, C)
    out = lax.all_to_all(out, "section", 0, 0, tiled=True)
    return out.transpose(1, 4, 2, 0, 3).reshape(share, C, 3, LAYERS * STRIP)


def solution(mesh):
    placed = (
        P(None, None, "tile", None),
        P("section", None),
        P("section", None, None, None),
        P("section", None),
    )
    return jax.shard_map(
        on_device,
        mesh=mesh,
        in_specs=placed,
        out_specs=P("section", None, "tile", None),
        check_vma=False,
    )
```

time: 553 us -> 362 us (0.65)
  waiting for transfers between devices: 266 us -> 85.1 us
  Pallas kernels: 0 us -> 141 us
  starting transfers between devices: 160 us -> 61.7 us
  other arithmetic: 37.8 us -> 2.92 us
  blocking collectives: 0 us -> 18.7 us
  local copies, waits for them, and re-layouts: 53.2 us -> 36.9 us
  matrix products: 14.9 us -> 0 us
    pallas_call x0 -> x8, Pallas kernels: none -> 141 us  [run_layer(): pl.pallas_call(functools.partial(layer_kernel, win), grid=(1,), out_shape...]
    psum x1 -> x0, waiting for transfers between devices: 113 us -> none  [broadcast(): return lax.psum(block, axis)]
    ppermute x33 -> x23, starting transfers between devices: 160 us -> 61.7 us  [the longest x8 26.8 us: on_device(): top = lax.ppermute(rows[2], 'tile', down)]
    ppermute x33 -> x23, waiting for transfers between devices: 153 us -> 55.9 us  [the longest x8 46.3 us: on_device(): bot = lax.ppermute(rows[0], 'tile', up)]
    all_gather x0 -> x2, waiting for transfers between devices: none -> 29.2 us  [the longest x1 29.2 us: on_device(): early = lax.all_gather(pieces[:FIRST, :PIECE], 'tile')]
    unnamed x5 -> x70, local copies, waits for them, and re-layouts: 4.31 us -> 30.4 us
    cond x84 -> x0, local copies, waits for them, and re-layouts: 20.3 us -> none
    all_to_all x0 -> x1, blocking collectives: none -> 18.7 us  [on_device(): out = lax.all_to_all(out, 'section', 0, 0, tiled=True)]
  transfers between devices with their start and end apart: 34 -> 25, of which waited for: 34 -> 18; matrix products, arithmetic and copies ran while one was open for 2% -> 3% of each run, Pallas kernels for 0% -> 11%
where the time goes in v1:
time: 362 us; the launch traced here: 360 us
  Pallas kernels  141 us (39%)
  waiting for transfers between devices  85.1 us (24%)
  starting transfers between devices  61.7 us (17%)
  local copies, waits for them, and re-layouts  36.9 us (10%)
  blocking collectives  18.7 us (5%)
  between operations  13.8 us (4%)
    pallas_call x8, Pallas kernels, run_layer(): pl.pallas_call(functools.partial(layer_kernel, win), grid=(1,), out_shape...  141 us
    ppermute x8, waiting for transfers between devices, on_device(): bot = lax.ppermute(rows[0], 'tile', up)  46.3 us
    unnamed x70, local copies, waits for them, and re-layouts  30.4 us
    all_gather x1, waiting for transfers between devices, on_device(): early = lax.all_gather(pieces[:FIRST, :PIECE], 'tile')  29.2 us
    ppermute x8, starting transfers between devices, on_device(): top = lax.ppermute(rows[2], 'tile', down)  26.8 us
    all_to_all x1, blocking collectives, on_device(): out = lax.all_to_all(out, 'section', 0, 0, tiled=True)  18.7 us
    ppermute x8, starting transfers between devices, on_device(): bot = lax.ppermute(rows[0], 'tile', up)  18.3 us
    ppermute x7, starting transfers between devices, on_device(): lax.ppermute(piece, 'section', [(i, (i + k) % LAYERS) for i in range(LAYE...  16.7 us
  transfers between devices with their start and end apart: 25, of which 18 were waited for; matrix products, arithmetic and copies ran while one was open for 3% of the time, Pallas kernels for 11%

profile of v1, /device:TPU:7, one launch (start us, length us, event | category | flops | bytes accessed | tf_op | source)
XLA Modules:
  0.0 360.3 jit_solution(10754016431539333302)
XLA Ops:
  6.5 1.7 copy-done
  10.2 1.7 collective-permute-start.2
  11.9 3.0 collective-permute-start.3
  14.9 3.8 %collective-permute-start.4 = (bf16[304,128]{1,0:T(8,128)(2,1)S(1)}, bf16[304,128]{1,0:T(8,128)(2,1)}, u32[]{:S(2)}, u32[]{:S(2)}) collective-permute-start(bf16[304,128]{1,0:T(8,128)(2,1)S(1)} %get-tuple-element.54), channel_id=1, source_target_pairs={{0,96},{32,128},{64,160},{96,192},{128,224},{160,0},{192,32},{224,... | collective-permute-start | bytes 233480 | tf_op jit(solution)/shard_map/ppermute | solution.py:146
  19.1 4.5 %collective-permute-start.6 = (bf16[304,128]{1,0:T(8,128)(2,1)S(1)}, bf16[304,128]{1,0:T(8,128)(2,1)S(1)}, u32[]{:S(2)}, u32[]{:S(2)}) collective-permute-start(bf16[304,128]{1,0:T(8,128)(2,1)S(1)} %get-tuple-element.54), channel_id=1, source_target_pairs={{0,160},{32,192},{64,224},{96,0},{128,32},{160,64},{192,96},{224,1... | collective-permute-start | bytes 233480 | tf_op jit(solution)/shard_map/ppermute | solution.py:146
  23.6 2.5 collective-permute-start.7
  29.7 5.8 %collective-permute-done.7 = bf16[304,128]{1,0:T(8,128)(2,1)S(1)} collective-permute-done((bf16[304,128]{1,0:T(8,128)(2,1)S(1)}, bf16[304,128]{1,0:T(8,128)(2,1)S(1)}, u32[]{:S(2)}, u32[]{:S(2)}) %collective-permute-start.7) | collective-permute-done | bytes 77856 | tf_op jit(solution)/shard_map/ppermute | solution.py:146
  35.7 1.5 gather_fusion
  37.2 1.2 broadcast_select_fusion
  40.0 4.9 %copy.11 = bf16[16,192,3,128]{1,0,3,2:T(8,128)(2,1)} copy(bf16[16,192,3,128]{3,1,2,0:T(8,128)(2,1)} %param.4) | data formatting | bytes 4718592 | tf_op args[0]
  44.9 1.2 fusion
  46.3 4.2 %collective-permute-start = (bf16[32,16,256]{2,1,0:T(8,128)(2,1)S(1)}, bf16[32,16,256]{2,1,0:T(8,128)(2,1)}, u32[]{:S(2)}, u32[]{:S(2)}) collective-permute-start(bf16[32,16,256]{2,1,0:T(8,128)(2,1)S(1)} %get-tuple-element.57.r2_ref), channel_id=1, source_target_pairs={{0,1},{1,2},{2,3},{3,4},{4,5},{5,6},{6,7},{7,8},{8,9},{9,10},{10,1... | collective-permute-start | bytes 786440 | tf_op jit(solution)/shard_map/ppermute | solution.py:167
  50.5 1.9 collective-permute-start.1
  54.6 6.8 %collective-permute-done.1.bot_ref = bf16[32,16,256]{2,1,0:T(8,128)(2,1)} collective-permute-done((bf16[32,16,256]{2,1,0:T(8,128)(2,1)S(1)}, bf16[32,16,256]{2,1,0:T(8,128)(2,1)}, u32[]{:S(2)}, u32[]{:S(2)}) %collective-permute-start.1) | collective-permute-done | bytes 262176 | tf_op jit(solution)/shard_map/ppermute | solution.py:168
  61.4 29.2 %all-gather.5.cloned.1.call-done = bf16[64,288,128]{2,1,0:T(8,128)(2,1)} async-done(((bf16[2,288,128]{2,1,0:T(8,128)(2,1)}), bf16[64,288,128]{2,1,0:T(8,128)(2,1)}) %all-gather.5.cloned.1.call-update) | async-done | bytes 4718608 | tf_op jit(solution)/shard_map/all_gather | solution.py:156
  90.6 2.3 copy-done.21
  93.0 21.5 %shard_map.46 = (bf16[30,16,256]{2,1,0:T(8,128)(2,1)}, bf16[30,16,256]{2,1,0:T(8,128)(2,1)S(1)}, bf16[30,16,256]{2,1,0:T(8,128)(2,1)}) custom-call(s32[1]{0:T(128)} %bitcast.7.base_ref, bf16[32,16,256]{2,1,0:T(8,128)(2,1)} %collective-permute-done.top_ref, bf16[32,16,256]{2,1,0:T(8,128)(2,1)S(1)} %get-tuple-element.56.r0_ref, ...), custom_call_target="tpu_custom_call" | custom-call | flops 2866544640 | bytes 4194304 | tf_op jit(solution)/shard_map/pallas_call | solution.py:113
  115.2 2.2 collective-permute-start.10
  117.4 5.7 %collective-permute-start.9 = (bf16[30,16,256]{2,1,0:T(8,128)(2,1)}, bf16[30,16,256]{2,1,0:T(8,128)(2,1)S(1)}, u32[]{:S(2)}, u32[]{:S(2)}) collective-permute-start(bf16[30,16,256]{2,1,0:T(8,128)(2,1)} %get-tuple-element.29.r2_ref), channel_id=1, source_target_pairs={{0,1},{1,2},{2,3},{3,4},{4,5},{5,6},{6,7},{7,8},{8,9},{9,10},{10,1... | collective-permute-start | bytes 737288 | tf_op jit(solution)/shard_map/ppermute | solution.py:167
  123.0 2.0 collective-permute-done.10.bot_ref
  127.0 2.3 copy-done.22
  131.3 1.1 copy-done.28
  132.4 19.6 %shard_map.47 = (bf16[28,16,256]{2,1,0:T(8,128)(2,1)S(1)}, bf16[28,16,256]{2,1,0:T(8,128)(2,1)S(1)}, bf16[28,16,256]{2,1,0:T(8,128)(2,1)S(1)}) custom-call(s32[1]{0:T(128)} %bitcast.6.base_ref, bf16[30,16,256]{2,1,0:T(8,128)(2,1)S(1)} %copy-done.26, bf16[30,16,256]{2,1,0:T(8,128)(2,1)} %get-tuple-element.30.r0_ref, bf16[30,16,256]{2,1,0:T(8,128)(2,1)S(1)} %copy-done.28, ...), custom_call_target="tpu_custom_call" | custom-call | flops 2675441664 | bytes 4194304 | tf_op jit(solution)/shard_map/pallas_call | solution.py:113
  152.0 7.4 %collective-permute-start.11 = (bf16[28,16,256]{2,1,0:T(8,128)(2,1)S(1)}, bf16[28,16,256]{2,1,0:T(8,128)(2,1)}, u32[]{:S(2)}, u32[]{:S(2)}) collective-permute-start(bf16[28,16,256]{2,1,0:T(8,128)(2,1)S(1)} %get-tuple-element.32.r2_ref), channel_id=1, source_target_pairs={{0,1},{1,2},{2,3},{3,4},{4,5},{5,6},{6,7},{7,8},{8,9},{9,10},{10,1... | collective-permute-start | bytes 688136 | tf_op jit(solution)/shard_map/ppermute | solution.py:167
  159.4 1.9 collective-permute-start.12
  162.3 6.6 %collective-permute-done.12.bot_ref = bf16[28,16,256]{2,1,0:T(8,128)(2,1)} collective-permute-done((bf16[28,16,256]{2,1,0:T(8,128)(2,1)S(1)}, bf16[28,16,256]{2,1,0:T(8,128)(2,1)}, u32[]{:S(2)}, u32[]{:S(2)}) %collective-permute-start.12) | collective-permute-done | bytes 229408 | tf_op jit(solution)/shard_map/ppermute | solution.py:168
  170.2 20.0 %shard_map.48 = (bf16[26,16,256]{2,1,0:T(8,128)(2,1)S(1)}, bf16[26,16,256]{2,1,0:T(8,128)(2,1)S(1)}, bf16[26,16,256]{2,1,0:T(8,128)(2,1)}) custom-call(s32[1]{0:T(128)} %bitcast.5.base_ref, bf16[28,16,256]{2,1,0:T(8,128)(2,1)} %collective-permute-done.11.top_ref, bf16[28,16,256]{2,1,0:T(8,128)(2,1)S(1)} %get-tuple-element.33.r0_ref, ...), custom_call_target="tpu_custom_call" | custom-call | flops 2484338688 | bytes 4194304 | tf_op jit(solution)/shard_map/pallas_call | solution.py:113
  190.9 1.9 collective-permute-start.13
  192.8 2.4 collective-permute-start.14
  195.9 6.2 %collective-permute-done.14.bot_ref = bf16[26,16,256]{2,1,0:T(8,128)(2,1)S(1)} collective-permute-done((bf16[26,16,256]{2,1,0:T(8,128)(2,1)S(1)}, bf16[26,16,256]{2,1,0:T(8,128)(2,1)S(1)}, u32[]{:S(2)}, u32[]{:S(2)}) %collective-permute-start.14) | collective-permute-done | bytes 213024 | tf_op jit(solution)/shard_map/ppermute | solution.py:168
  204.3 18.6 %shard_map.49 = (bf16[24,16,256]{2,1,0:T(8,128)(2,1)S(1)}, bf16[24,16,256]{2,1,0:T(8,128)(2,1)S(1)}, bf16[24,16,256]{2,1,0:T(8,128)(2,1)}) custom-call(s32[1]{0:T(128)} %bitcast.4.base_ref, bf16[26,16,256]{2,1,0:T(8,128)(2,1)S(1)} %collective-permute-done.13.top_ref, bf16[26,16,256]{2,1,0:T(8,128)(2,1)S(1)} %get-tuple-element.36.r0_ref, ...), custom_call_target="tpu_custom_call" | custom-call | flops 2293235712 | bytes 4194304 | tf_op jit(solution)/shard_map/pallas_call | solution.py:113
  223.6 1.9 collective-permute-start.15
  225.5 2.6 collective-permute-start.16
  228.4 6.2 %collective-permute-done.16.bot_ref = bf16[24,16,256]{2,1,0:T(8,128)(2,1)S(1)} collective-permute-done((bf16[24,16,256]{2,1,0:T(8,128)(2,1)S(1)}, bf16[24,16,256]{2,1,0:T(8,128)(2,1)S(1)}, u32[]{:S(2)}, u32[]{:S(2)}) %collective-permute-start.16) | collective-permute-done | bytes 196640 | tf_op jit(solution)/shard_map/ppermute | solution.py:168
  236.9 17.4 %shard_map.50 = (bf16[22,16,256]{2,1,0:T(8,128)(2,1)S(1)}, bf16[22,16,256]{2,1,0:T(8,128)(2,1)S(1)}, bf16[22,16,256]{2,1,0:T(8,128)(2,1)}) custom-call(s32[1]{0:T(128)} %bitcast.3.base_ref, bf16[24,16,256]{2,1,0:T(8,128)(2,1)S(1)} %collective-permute-done.15.top_ref, bf16[24,16,256]{2,1,0:T(8,128)(2,1)S(1)} %get-tuple-element.39.r0_ref, ...), custom_call_target="tpu_custom_call" | custom-call | flops 2102132736 | bytes 4194304 | tf_op jit(solution)/shard_map/pallas_call | solution.py:113
  254.9 1.9 collective-permute-start.17
  256.9 2.4 collective-permute-start.18
  259.6 6.2 %collective-permute-done.18.bot_ref = bf16[22,16,256]{2,1,0:T(8,128)(2,1)S(1)} collective-permute-done((bf16[22,16,256]{2,1,0:T(8,128)(2,1)S(1)}, bf16[22,16,256]{2,1,0:T(8,128)(2,1)S(1)}, u32[]{:S(2)}, u32[]{:S(2)}) %collective-permute-start.18) | collective-permute-done | bytes 180256 | tf_op jit(solution)/shard_map/ppermute | solution.py:168
  266.7 16.1 %shard_map.51 = (bf16[20,16,256]{2,1,0:T(8,128)(2,1)S(1)}, bf16[20,16,256]{2,1,0:T(8,128)(2,1)S(1)}, bf16[20,16,256]{2,1,0:T(8,128)(2,1)}) custom-call(s32[1]{0:T(128)} %bitcast.2.base_ref, bf16[22,16,256]{2,1,0:T(8,128)(2,1)S(1)} %collective-permute-done.17.top_ref, bf16[22,16,256]{2,1,0:T(8,128)(2,1)S(1)} %get-tuple-element.42.r0_ref, ...), custom_call_target="tpu_custom_call" | custom-call | flops 1911029760 | bytes 4194304 | tf_op jit(solution)/shard_map/pallas_call | solution.py:113
  283.5 1.9 collective-permute-start.19
  285.4 2.4 collective-permute-start.20
  288.0 6.2 %collective-permute-done.20.bot_ref = bf16[20,16,256]{2,1,0:T(8,128)(2,1)S(1)} collective-permute-done((bf16[20,16,256]{2,1,0:T(8,128)(2,1)S(1)}, bf16[20,16,256]{2,1,0:T(8,128)(2,1)S(1)}, u32[]{:S(2)}, u32[]{:S(2)}) %collective-permute-start.20) | collective-permute-done | bytes 163872 | tf_op jit(solution)/shard_map/ppermute | solution.py:168
  295.1 14.9 %shard_map.52 = (bf16[18,16,256]{2,1,0:T(8,128)(2,1)S(1)}, bf16[18,16,256]{2,1,0:T(8,128)(2,1)S(1)}, bf16[18,16,256]{2,1,0:T(8,128)(2,1)}) custom-call(s32[1]{0:T(128)} %bitcast.1.base_ref, bf16[20,16,256]{2,1,0:T(8,128)(2,1)S(1)} %collective-permute-done.19.top_ref, bf16[20,16,256]{2,1,0:T(8,128)(2,1)S(1)} %get-tuple-element.45.r0_ref, ...), custom_call_target="tpu_custom_call" | custom-call | flops 1719926784 | bytes 4194304 | tf_op jit(solution)/shard_map/pallas_call | solution.py:113
  310.0 1.9 collective-permute-start.21
  311.9 2.4 collective-permute-start.22
  314.4 6.1 %collective-permute-done.22.bot_ref = bf16[18,16,256]{2,1,0:T(8,128)(2,1)S(1)} collective-permute-done((bf16[18,16,256]{2,1,0:T(8,128)(2,1)S(1)}, bf16[18,16,256]{2,1,0:T(8,128)(2,1)S(1)}, u32[]{:S(2)}, u32[]{:S(2)}) %collective-permute-start.22) | collective-permute-done | bytes 147488 | tf_op jit(solution)/shard_map/ppermute | solution.py:168
  320.5 13.0 %shard_map.53 = (bf16[16,16,256]{2,1,0:T(8,128)(2,1)S(1)}, bf16[16,16,256]{2,1,0:T(8,128)(2,1)S(1)}, bf16[16,16,256]{2,1,0:T(8,128)(2,1)S(1)}) custom-call(s32[1]{0:T(128)} %bitcast.base_ref, bf16[18,16,256]{2,1,0:T(8,128)(2,1)S(1)} %collective-permute-done.21.top_ref, bf16[18,16,256]{2,1,0:T(8,128)(2,1)S(1)} %get-tuple-element.48.r0_ref, ...), custom_call_target="tpu_custom_call" | custom-call | flops 1528823808 | bytes 4194304 | tf_op jit(solution)/shard_map/pallas_call | solution.py:113
  333.8 18.7 %all_to_all.5 = bf16[8,2,3,16,192]{4,3,2,1,0:T(8,128)(2,1)S(1)} all-to-all(bf16[8,2,3,16,192]{4,3,2,1,0:T(8,128)(2,1)S(1)} %bitcast.100), channel_id=1, replica_groups=mesh['section'=8,'tile'=32] {'section'}, dimensions={0} | all-to-all | bytes 589824 | tf_op jit(solution)/shard_map/all_to_all | solution.py:179
  (115 shorter events, 28.6 us)
Async XLA Ops:
  6.5 1.8 copy-start
  6.5 84.1 %all-gather.5.cloned.1.call-start = ((), (), s32[]{:S(2)}) async-start(), calls=%async_computation.1 | async-start | bytes 4866048 | tf_op jit(solution)/shard_map/all_gather | solution.py:156
  10.2 13.4 %collective-permute-start.2 = (bf16[304,128]{1,0:T(8,128)(2,1)S(1)}, bf16[304,128]{1,0:T(8,128)(2,1)}, u32[]{:S(2)}, u32[]{:S(2)}) collective-permute-start(bf16[304,128]{1,0:T(8,128)(2,1)S(1)} %get-tuple-element.54), channel_id=1, source_target_pairs={{0,32},{32,64},{64,96},{96,128},{128,160},{160,192},{192,224},{224... | collective-permute-start | bytes 233480 | tf_op jit(solution)/shard_map/ppermute | solution.py:146
  11.9 15.1 %collective-permute-start.3 = (bf16[304,128]{1,0:T(8,128)(2,1)S(1)}, bf16[304,128]{1,0:T(8,128)(2,1)}, u32[]{:S(2)}, u32[]{:S(2)}) collective-permute-start(bf16[304,128]{1,0:T(8,128)(2,1)S(1)} %get-tuple-element.54), channel_id=1, source_target_pairs={{0,64},{32,96},{64,128},{96,160},{128,192},{160,224},{192,0},{224,... | collective-permute-start | bytes 233480 | tf_op jit(solution)/shard_map/ppermute | solution.py:146
  14.9 13.8 %collective-permute-start.4 = (bf16[304,128]{1,0:T(8,128)(2,1)S(1)}, bf16[304,128]{1,0:T(8,128)(2,1)}, u32[]{:S(2)}, u32[]{:S(2)}) collective-permute-start(bf16[304,128]{1,0:T(8,128)(2,1)S(1)} %get-tuple-element.54), channel_id=1, source_target_pairs={{0,96},{32,128},{64,160},{96,192},{128,224},{160,0},{192,32},{224,... | collective-permute-start | bytes 233480 | tf_op jit(solution)/shard_map/ppermute | solution.py:146
  18.6 11.0 %collective-permute-start.5 = (bf16[304,128]{1,0:T(8,128)(2,1)S(1)}, bf16[304,128]{1,0:T(8,128)(2,1)S(1)}, u32[]{:S(2)}, u32[]{:S(2)}) collective-permute-start(bf16[304,128]{1,0:T(8,128)(2,1)S(1)} %get-tuple-element.54), channel_id=1, source_target_pairs={{0,128},{32,160},{64,192},{96,224},{128,0},{160,32},{192,64},{224,... | collective-permute-start | bytes 233480 | tf_op jit(solution)/shard_map/ppermute | solution.py:146
  19.1 10.5 %collective-permute-start.6 = (bf16[304,128]{1,0:T(8,128)(2,1)S(1)}, bf16[304,128]{1,0:T(8,128)(2,1)S(1)}, u32[]{:S(2)}, u32[]{:S(2)}) collective-permute-start(bf16[304,128]{1,0:T(8,128)(2,1)S(1)} %get-tuple-element.54), channel_id=1, source_target_pairs={{0,160},{32,192},{64,224},{96,0},{128,32},{160,64},{192,96},{224,1... | collective-permute-start | bytes 233480 | tf_op jit(solution)/shard_map/ppermute | solution.py:146
  23.6 11.8 %collective-permute-start.7 = (bf16[304,128]{1,0:T(8,128)(2,1)S(1)}, bf16[304,128]{1,0:T(8,128)(2,1)S(1)}, u32[]{:S(2)}, u32[]{:S(2)}) collective-permute-start(bf16[304,128]{1,0:T(8,128)(2,1)S(1)} %get-tuple-element.54), channel_id=1, source_target_pairs={{0,192},{32,224},{64,0},{96,32},{128,64},{160,96},{192,128},{224,1... | collective-permute-start | bytes 233480 | tf_op jit(solution)/shard_map/ppermute | solution.py:146
  27.0 8.7 %collective-permute-start.8 = (bf16[304,128]{1,0:T(8,128)(2,1)S(1)}, bf16[304,128]{1,0:T(8,128)(2,1)S(1)}, u32[]{:S(2)}, u32[]{:S(2)}) collective-permute-start(bf16[304,128]{1,0:T(8,128)(2,1)S(1)} %get-tuple-element.54), channel_id=1, source_target_pairs={{0,224},{32,0},{64,32},{96,64},{128,96},{160,128},{192,160},{224,1... | collective-permute-start | bytes 233480 | tf_op jit(solution)/shard_map/ppermute | solution.py:146
  38.4 6.6 %copy-start.29 = (bf16[8,304,128]{2,1,0:T(8,128)(2,1)}, bf16[8,304,128]{2,1,0:T(8,128)(2,1)S(1)}, u32[]{:S(2)}) copy-start(bf16[8,304,128]{2,1,0:T(8,128)(2,1)S(1)} %broadcast_select_fusion) | copy-start | bytes 1867780
  39.1 129.8 %all-gather.7.cloned.1.call-start = ((), (), s32[]{:S(2)}) async-start(), calls=%async_computation.2 | async-start | bytes 14598144 | tf_op jit(solution)/shard_map/all_gather | solution.py:157
  46.3 8.3 %collective-permute-start = (bf16[32,16,256]{2,1,0:T(8,128)(2,1)S(1)}, bf16[32,16,256]{2,1,0:T(8,128)(2,1)}, u32[]{:S(2)}, u32[]{:S(2)}) collective-permute-start(bf16[32,16,256]{2,1,0:T(8,128)(2,1)S(1)} %get-tuple-element.57.r2_ref), channel_id=1, source_target_pairs={{0,1},{1,2},{2,3},{3,4},{4,5},{5,6},{6,7},{7,8},{8,9},{9,10},{10,1... | collective-permute-start | bytes 786440 | tf_op jit(solution)/shard_map/ppermute | solution.py:167
  50.5 10.9 %collective-permute-start.1 = (bf16[32,16,256]{2,1,0:T(8,128)(2,1)S(1)}, bf16[32,16,256]{2,1,0:T(8,128)(2,1)}, u32[]{:S(2)}, u32[]{:S(2)}) collective-permute-start(bf16[32,16,256]{2,1,0:T(8,128)(2,1)S(1)} %get-tuple-element.56.r0_ref), channel_id=1, source_target_pairs={{1,0},{2,1},{3,2},{4,3},{5,4},{6,5},{7,6},{8,7},{9,8},{10,9},{11,1... | collective-permute-start | bytes 786440 | tf_op jit(solution)/shard_map/ppermute | solution.py:168
  90.6 2.3 copy-start.21
  114.5 0.7 copy-start.27
  115.2 9.8 %collective-permute-start.10 = (bf16[30,16,256]{2,1,0:T(8,128)(2,1)}, bf16[30,16,256]{2,1,0:T(8,128)(2,1)S(1)}, u32[]{:S(2)}, u32[]{:S(2)}) collective-permute-start(bf16[30,16,256]{2,1,0:T(8,128)(2,1)} %get-tuple-element.30.r0_ref), channel_id=1, source_target_pairs={{1,0},{2,1},{3,2},{4,3},{5,4},{6,5},{7,6},{8,7},{9,8},{10,9},{11,1... | collective-permute-start | bytes 737288 | tf_op jit(solution)/shard_map/ppermute | solution.py:168
  117.4 8.9 %collective-permute-start.9 = (bf16[30,16,256]{2,1,0:T(8,128)(2,1)}, bf16[30,16,256]{2,1,0:T(8,128)(2,1)S(1)}, u32[]{:S(2)}, u32[]{:S(2)}) collective-permute-start(bf16[30,16,256]{2,1,0:T(8,128)(2,1)} %get-tuple-element.29.r2_ref), channel_id=1, source_target_pairs={{0,1},{1,2},{2,3},{3,4},{4,5},{5,6},{6,7},{7,8},{8,9},{9,10},{10,1... | collective-permute-start | bytes 737288 | tf_op jit(solution)/shard_map/ppermute | solution.py:167
  125.0 0.7 copy-start.23
  126.3 0.7 copy-start.25
  127.0 2.3 copy-start.22
  129.3 0.9 copy-start.24
  130.3 1.0 copy-start.26
  131.3 1.1 copy-start.28
  152.0 10.3 %collective-permute-start.11 = (bf16[28,16,256]{2,1,0:T(8,128)(2,1)S(1)}, bf16[28,16,256]{2,1,0:T(8,128)(2,1)}, u32[]{:S(2)}, u32[]{:S(2)}) collective-permute-start(bf16[28,16,256]{2,1,0:T(8,128)(2,1)S(1)} %get-tuple-element.32.r2_ref), channel_id=1, source_target_pairs={{0,1},{1,2},{2,3},{3,4},{4,5},{5,6},{6,7},{7,8},{8,9},{9,10},{10,1... | collective-permute-start | bytes 688136 | tf_op jit(solution)/shard_map/ppermute | solution.py:167
  159.4 9.6 %collective-permute-start.12 = (bf16[28,16,256]{2,1,0:T(8,128)(2,1)S(1)}, bf16[28,16,256]{2,1,0:T(8,128)(2,1)}, u32[]{:S(2)}, u32[]{:S(2)}) collective-permute-start(bf16[28,16,256]{2,1,0:T(8,128)(2,1)S(1)} %get-tuple-element.33.r0_ref), channel_id=1, source_target_pairs={{1,0},{2,1},{3,2},{4,3},{5,4},{6,5},{7,6},{8,7},{9,8},{10,9},{11,1... | collective-permute-start | bytes 688136 | tf_op jit(solution)/shard_map/ppermute | solution.py:168
  190.2 0.7 copy-start.1
  190.9 5.0 %collective-permute-start.13 = (bf16[26,16,256]{2,1,0:T(8,128)(2,1)}, bf16[26,16,256]{2,1,0:T(8,128)(2,1)S(1)}, u32[]{:S(2)}, u32[]{:S(2)}) collective-permute-start(bf16[26,16,256]{2,1,0:T(8,128)(2,1)} %get-tuple-element.35.r2_ref), channel_id=1, source_target_pairs={{0,1},{1,2},{2,3},{3,4},{4,5},{5,6},{6,7},{7,8},{8,9},{9,10},{10,1... | collective-permute-start | bytes 638984 | tf_op jit(solution)/shard_map/ppermute | solution.py:167
  192.8 9.3 %collective-permute-start.14 = (bf16[26,16,256]{2,1,0:T(8,128)(2,1)S(1)}, bf16[26,16,256]{2,1,0:T(8,128)(2,1)S(1)}, u32[]{:S(2)}, u32[]{:S(2)}) collective-permute-start(bf16[26,16,256]{2,1,0:T(8,128)(2,1)S(1)} %get-tuple-element.36.r0_ref), channel_id=1, source_target_pairs={{1,0},{2,1},{3,2},{4,3},{5,4},{6,5},{7,6},{8,7},{9,8},{10,9},{11,1... | collective-permute-start | bytes 638984 | tf_op jit(solution)/shard_map/ppermute | solution.py:168
  202.1 0.9 copy-start.2
  203.0 0.7 copy-start.17
  222.9 0.7 copy-start.3
  223.6 4.8 %collective-permute-start.15 = (bf16[24,16,256]{2,1,0:T(8,128)(2,1)}, bf16[24,16,256]{2,1,0:T(8,128)(2,1)S(1)}, u32[]{:S(2)}, u32[]{:S(2)}) collective-permute-start(bf16[24,16,256]{2,1,0:T(8,128)(2,1)} %get-tuple-element.38.r2_ref), channel_id=1, source_target_pairs={{0,1},{1,2},{2,3},{3,4},{4,5},{5,6},{6,7},{7,8},{8,9},{9,10},{10,1... | collective-permute-start | bytes 589832 | tf_op jit(solution)/shard_map/ppermute | solution.py:167
  225.5 9.1 %collective-permute-start.16 = (bf16[24,16,256]{2,1,0:T(8,128)(2,1)S(1)}, bf16[24,16,256]{2,1,0:T(8,128)(2,1)S(1)}, u32[]{:S(2)}, u32[]{:S(2)}) collective-permute-start(bf16[24,16,256]{2,1,0:T(8,128)(2,1)S(1)} %get-tuple-element.39.r0_ref), channel_id=1, source_target_pairs={{1,0},{2,1},{3,2},{4,3},{5,4},{6,5},{7,6},{8,7},{9,8},{10,9},{11,1... | collective-permute-start | bytes 589832 | tf_op jit(solution)/shard_map/ppermute | solution.py:168
  234.6 0.9 copy-start.4
  236.9 28.9 %copy-start.13 = (f32[1,256]{1,0:T(1,128)S(1)}, f32[1,256]{1,0:T(1,128)}, u32[]{:S(2)}) copy-start(f32[1,256]{1,0:T(1,128)} %get-tuple-element.64.bias_ref) | copy-start | bytes 3076
  236.9 28.9 %copy-start.14 = (f32[1,256]{1,0:T(1,128)S(1)}, f32[1,256]{1,0:T(1,128)}, u32[]{:S(2)}) copy-start(f32[1,256]{1,0:T(1,128)} %get-tuple-element.65.gain_ref) | copy-start | bytes 3076
  254.9 4.6 %collective-permute-start.17 = (bf16[22,16,256]{2,1,0:T(8,128)(2,1)}, bf16[22,16,256]{2,1,0:T(8,128)(2,1)S(1)}, u32[]{:S(2)}, u32[]{:S(2)}) collective-permute-start(bf16[22,16,256]{2,1,0:T(8,128)(2,1)} %get-tuple-element.41.r2_ref), channel_id=1, source_target_pairs={{0,1},{1,2},{2,3},{3,4},{4,5},{5,6},{6,7},{7,8},{8,9},{9,10},{10,1... | collective-permute-start | bytes 540680 | tf_op jit(solution)/shard_map/ppermute | solution.py:167
  256.9 8.9 %collective-permute-start.18 = (bf16[22,16,256]{2,1,0:T(8,128)(2,1)S(1)}, bf16[22,16,256]{2,1,0:T(8,128)(2,1)S(1)}, u32[]{:S(2)}, u32[]{:S(2)}) collective-permute-start(bf16[22,16,256]{2,1,0:T(8,128)(2,1)S(1)} %get-tuple-element.42.r0_ref), channel_id=1, source_target_pairs={{1,0},{2,1},{3,2},{4,3},{5,4},{6,5},{7,6},{8,7},{9,8},{10,9},{11,1... | collective-permute-start | bytes 540680 | tf_op jit(solution)/shard_map/ppermute | solution.py:168
  265.8 0.9 copy-start.6
  266.7 27.5 %copy-start.11 = (f32[1,256]{1,0:T(1,128)S(1)}, f32[1,256]{1,0:T(1,128)}, u32[]{:S(2)}) copy-start(f32[1,256]{1,0:T(1,128)} %get-tuple-element.62.bias_ref) | copy-start | bytes 3076
  266.7 27.5 %copy-start.12 = (f32[1,256]{1,0:T(1,128)S(1)}, f32[1,256]{1,0:T(1,128)}, u32[]{:S(2)}) copy-start(f32[1,256]{1,0:T(1,128)} %get-tuple-element.63.gain_ref) | copy-start | bytes 3076
  283.5 4.5 %collective-permute-start.19 = (bf16[20,16,256]{2,1,0:T(8,128)(2,1)}, bf16[20,16,256]{2,1,0:T(8,128)(2,1)S(1)}, u32[]{:S(2)}, u32[]{:S(2)}) collective-permute-start(bf16[20,16,256]{2,1,0:T(8,128)(2,1)} %get-tuple-element.44.r2_ref), channel_id=1, source_target_pairs={{0,1},{1,2},{2,3},{3,4},{4,5},{5,6},{6,7},{7,8},{8,9},{9,10},{10,1... | collective-permute-start | bytes 491528 | tf_op jit(solution)/shard_map/ppermute | solution.py:167
  285.4 8.7 %collective-permute-start.20 = (bf16[20,16,256]{2,1,0:T(8,128)(2,1)S(1)}, bf16[20,16,256]{2,1,0:T(8,128)(2,1)S(1)}, u32[]{:S(2)}, u32[]{:S(2)}) collective-permute-start(bf16[20,16,256]{2,1,0:T(8,128)(2,1)S(1)} %get-tuple-element.45.r0_ref), channel_id=1, source_target_pairs={{1,0},{2,1},{3,2},{4,3},{5,4},{6,5},{7,6},{8,7},{9,8},{10,9},{11,1... | collective-permute-start | bytes 491528 | tf_op jit(solution)/shard_map/ppermute | solution.py:168
  294.2 0.9 copy-start.8
  295.1 25.4 %copy-start.9 = (f32[1,256]{1,0:T(1,128)S(1)}, f32[1,256]{1,0:T(1,128)}, u32[]{:S(2)}) copy-start(f32[1,256]{1,0:T(1,128)} %get-tuple-element.60.bias_ref) | copy-start | bytes 3076
  295.1 25.4 %copy-start.10 = (f32[1,256]{1,0:T(1,128)S(1)}, f32[1,256]{1,0:T(1,128)}, u32[]{:S(2)}) copy-start(f32[1,256]{1,0:T(1,128)} %get-tuple-element.61.gain_ref) | copy-start | bytes 3076
  310.0 4.3 %collective-permute-start.21 = (bf16[18,16,256]{2,1,0:T(8,128)(2,1)}, bf16[18,16,256]{2,1,0:T(8,128)(2,1)S(1)}, u32[]{:S(2)}, u32[]{:S(2)}) collective-permute-start(bf16[18,16,256]{2,1,0:T(8,128)(2,1)} %get-tuple-element.47.r2_ref), channel_id=1, source_target_pairs={{0,1},{1,2},{2,3},{3,4},{4,5},{5,6},{6,7},{7,8},{8,9},{9,10},{10,1... | collective-permute-start | bytes 442376 | tf_op jit(solution)/shard_map/ppermute | solution.py:167
  311.9 8.6 %collective-permute-start.22 = (bf16[18,16,256]{2,1,0:T(8,128)(2,1)S(1)}, bf16[18,16,256]{2,1,0:T(8,128)(2,1)S(1)}, u32[]{:S(2)}, u32[]{:S(2)}) collective-permute-start(bf16[18,16,256]{2,1,0:T(8,128)(2,1)S(1)} %get-tuple-element.48.r0_ref), channel_id=1, source_target_pairs={{1,0},{2,1},{3,2},{4,3},{5,4},{6,5},{7,6},{8,7},{9,8},{10,9},{11,1... | collective-permute-start | bytes 442376 | tf_op jit(solution)/shard_map/ppermute | solution.py:168
  (7 other events, 4.6 us)
Sparse Core Ops, SparseCore 0:
  39.3 51.3 all-gather.4
  93.2 71.7 all-gather.6
